TPU v7x, 128 devices: a whole 4x4x4 slice. The times are simulated.
128 devices in a mesh: row: 8 (over z_hi, x), col: 16 (over y, z_lo, core).
Axes of the slice: x: 4, y: 4, z: 4 (z_hi: 2, z_lo: 2; z = z_hi * 2 + z_lo), core: 2. Of those that a mesh axis runs over, the one named last changes fastest.
Arguments:
- pattern: int32 [32, 32], replicated, may hold values from 0 to 1, as said below
- matrix: bfloat16 [4096, 4096], P('row', 'col'), as said below
Outputs:
- sign_estimate: float32 [4096, 4096], P('row', 'col')
Inputs may be any that keep to these rules, and one draw needn't show every extreme that they name: pattern is symmetric, its diagonal is 1, a kept block joins cells at squared distance 5 or less, no block row keeps more than 26 blocks, and some block row keeps exactly 26. matrix is symmetric and zero in every block where pattern is 0.
All inputs are finite; a program needn't handle non-finite values.
Results may differ from a plain program's by a relative error of at most 0.027.
Values may be sent and summed in bfloat16 or wider, within the bound.
A program may use at most 64 MiB of HBM per device.

v0:
```python
import jax
import jax.numpy as jnp
from jax import lax
from jax.sharding import PartitionSpec as P

BLOCK = 128
ITERS = 2


def contract(left_part, right_part):
    return jnp.dot(left_part, right_part, preferred_element_type=jnp.float32)


def shards(pattern, matrix):
    br_count = matrix.shape[0] // BLOCK
    bc_count = matrix.shape[1] // BLOCK
    row_place = lax.axis_index("row")
    col_place = lax.axis_index("col")
    tile_mask = lax.dynamic_slice(
        pattern, (row_place * br_count, col_place * bc_count), (br_count, bc_count)
    )
    expanded = jnp.repeat(jnp.repeat(tile_mask.astype(jnp.float32), BLOCK, axis=0), BLOCK, axis=1)
    current = matrix
    for section in range(ITERS):
        columns = lax.all_gather(current, "row", axis=0, tiled=True)
        left_part = lax.all_gather(current, "col", axis=1, tiled=True)
        scale = 1.0 / (3.0 * columns.shape[0])
        raw_square = contract(left_part, columns)
        square = (raw_square * expanded * scale).astype(jnp.bfloat16)
        cube = contract(left_part, lax.all_gather(square, "row", axis=0, tiled=True))
        updated = expanded * (1.5 * current.astype(jnp.float32) - 0.5 * cube)
        if section + 1 < ITERS:
            current = updated.astype(jnp.bfloat16)
        else:
            current = updated
    return current


def solution(mesh):
    in_specs = (P(), P("row", "col"))
    out_specs = P("row", "col")
    return jax.shard_map(shards, mesh=mesh, in_specs=in_specs, out_specs=out_specs, check_vma=False)
```

profile of v0, /device:TPU:5, one launch (start us, length us, event | category | flops | bytes accessed | tf_op | source)
XLA Modules:
  0.0 346.2 jit_solution(13338555392073163860)
XLA Ops:
  6.5 0.0 all-gather.9.cloned.1.call-start
  6.5 0.7 all-gather.9.cloned.1.call-update
  7.3 0.0 all-gather.7.cloned.1.call-start
  7.3 0.7 all-gather.7.cloned.1.call-update
  8.0 0.0 all-gather.11.cloned.1.call-start
  8.1 0.8 dynamic-slice_convert_fusion
  8.8 0.1 copy.3
  8.9 0.1 broadcast_bitcast_fusion
  9.0 55.3 %all-gather.9.cloned.1.call-done = bf16[4096,256]{1,0:T(8,128)(2,1)} async-done(((bf16[512,256]{1,0:T(8,128)(2,1)}), bf16[4096,256]{1,0:T(8,128)(2,1)}) %all-gather.9.cloned.1.call-update) | async-done | bytes 2097168 | tf_op jit(solution)/shard_map/all_gather | solution.py:25
  64.3 48.2 %all-gather.7.cloned.1.call-done = bf16[512,4096]{1,0:T(8,128)(2,1)} async-done(((bf16[512,256]{1,0:T(8,128)(2,1)}), bf16[512,4096]{1,0:T(8,128)(2,1)}) %all-gather.7.cloned.1.call-update) | async-done | bytes 4194320 | tf_op jit(solution)/shard_map/all_gather | solution.py:26
  112.5 0.0 copy-start.1
  112.5 4.9 %fusion.6 = bf16[512,256]{0,1:T(8,128)(2,1)} fusion(bf16[512,4096]{1,0:T(8,128)(2,1)} %all-gather.7.cloned.1.call-done, bf16[4096,256]{1,0:T(8,128)(2,1)} %all-gather.9.cloned.1.call-done, f32[512,2]{0,1:T(2,128)S(1)} %bitcast.38), kind=kOutput, calls=%fused_computation.12 | convolution fusion | flops 1074135040 | bytes 6557696 | tf_op jit(solution)/shard_map/dot_general | solution.py:11
  117.4 0.0 all-gather.11.cloned.1.call-update
  117.4 0.0 all-gather.15.cloned.1.call-start
  117.4 0.0 copy-done.1
  117.5 0.1 copy.4
  117.6 55.2 %all-gather.11.cloned.1.call-done = bf16[4096,256]{0,1:T(8,128)(2,1)} async-done(((bf16[512,256]{0,1:T(8,128)(2,1)}), bf16[4096,256]{0,1:T(8,128)(2,1)}) %all-gather.11.cloned.1.call-update) | async-done | bytes 2097168 | tf_op jit(solution)/shard_map/all_gather | solution.py:30
  172.8 4.8 %fusion.7 = bf16[512,256]{0,1:T(8,128)(2,1)} fusion(bf16[4096,256]{0,1:T(8,128)(2,1)} %all-gather.11.cloned.1.call-done, bf16[512,4096]{1,0:T(8,128)(2,1)} %all-gather.7.cloned.1.call-done, bf16[512,256]{0,1:T(8,128)(2,1)S(1)} %copy.4, f32[512,2]{0,1:T(2,128)S(1)} %bitcast.39), kind=kOutput, calls=%fused_computation.13 | convolution fusion | flops 1074528256 | bytes 6819840 | tf_op jit(solution)/shard_map/dot_general | solution.py:11
  177.6 0.0 all-gather.15.cloned.1.call-update
  177.6 0.0 all-gather.13.cloned.1.call-start
  177.7 0.5 all-gather.13.cloned.1.call-update
  178.2 0.0 copy-start
  178.2 0.0 all-gather.17.cloned.1.call-start
  178.3 55.7 %all-gather.15.cloned.1.call-done = bf16[4096,256]{0,1:T(8,128)(2,1)} async-done(((bf16[512,256]{0,1:T(8,128)(2,1)}), bf16[4096,256]{0,1:T(8,128)(2,1)}) %all-gather.15.cloned.1.call-update) | async-done | bytes 2097168 | tf_op jit(solution)/shard_map/all_gather | solution.py:25
  234.0 40.4 %all-gather.13.cloned.1.call-done = bf16[512,4096]{0,1:T(8,128)(2,1)} async-done(((bf16[512,256]{0,1:T(8,128)(2,1)}), bf16[512,4096]{0,1:T(8,128)(2,1)}) %all-gather.13.cloned.1.call-update) | async-done | bytes 4194320 | tf_op jit(solution)/shard_map/all_gather | solution.py:26
  274.4 4.8 %fusion.5 = bf16[512,256]{0,1:T(8,128)(2,1)} fusion(bf16[4096,256]{0,1:T(8,128)(2,1)} %all-gather.15.cloned.1.call-done, bf16[512,4096]{0,1:T(8,128)(2,1)} %all-gather.13.cloned.1.call-done, f32[512,2]{0,1:T(2,128)S(1)} %bitcast.40), kind=kOutput, calls=%fused_computation.11 | convolution fusion | flops 1074135040 | bytes 6557696 | tf_op jit(solution)/shard_map/dot_general | solution.py:11
  279.2 0.0 all-gather.17.cloned.1.call-update
  279.2 55.0 %all-gather.17.cloned.1.call-done = bf16[4096,256]{0,1:T(8,128)(2,1)} async-done(((bf16[512,256]{0,1:T(8,128)(2,1)}), bf16[4096,256]{0,1:T(8,128)(2,1)}) %all-gather.17.cloned.1.call-update) | async-done | bytes 2097168 | tf_op jit(solution)/shard_map/all_gather | solution.py:30
  334.2 0.0 copy-done
  334.2 4.1 %bitcast_multiply_fusion = f32[512,256]{0,1:T(8,128)S(1)} fusion(bf16[4096,256]{0,1:T(8,128)(2,1)} %all-gather.17.cloned.1.call-done, bf16[512,4096]{0,1:T(8,128)(2,1)} %all-gather.13.cloned.1.call-done, bf16[512,256]{0,1:T(8,128)(2,1)S(1)} %copy-done, f32[512,2]{0,1:T(2,128)S(1)} %bitcast.41), kind=kOutput, calls=%fused_computation | convolution fusion | flops 1074397184 | bytes 7081984 | tf_op jit(solution)/shard_map/dot_general | solution.py:11
  338.3 1.0 copy.6
  (1 shorter events, 0.0 us)
Async XLA Ops:
  6.5 57.7 %all-gather.9.cloned.1.call-start = ((), (), s32[]{:S(2)}) async-start(), calls=%async_computation.1 | async-start | bytes 2359296 | tf_op jit(solution)/shard_map/all_gather | solution.py:25
  7.3 105.2 %all-gather.7.cloned.1.call-start = ((), (), s32[]{:S(2)}) async-start(), calls=%async_computation | async-start | bytes 4456448 | tf_op jit(solution)/shard_map/all_gather | solution.py:26
  8.0 164.8 %all-gather.11.cloned.1.call-start = ((), (), s32[]{:S(2)}) async-start(), calls=%async_computation.2 | async-start | bytes 2359296 | tf_op jit(solution)/shard_map/all_gather | solution.py:30
  112.5 5.0 %copy-start.1 = (bf16[512,256]{1,0:T(8,128)(2,1)S(1)}, bf16[512,256]{1,0:T(8,128)(2,1)}, u32[]{:S(2)}) copy-start(bf16[512,256]{1,0:T(8,128)(2,1)} %param.3) | copy-start | bytes 786436
  117.4 116.6 %all-gather.15.cloned.1.call-start = ((), (), s32[]{:S(2)}) async-start(), calls=%async_computation.4 | async-start | bytes 2359296 | tf_op jit(solution)/shard_map/all_gather | solution.py:25
  177.6 96.8 %all-gather.13.cloned.1.call-start = ((), (), s32[]{:S(2)}) async-start(), calls=%async_computation.3 | async-start | bytes 4456448 | tf_op jit(solution)/shard_map/all_gather | solution.py:26
  178.2 156.0 %copy-start = (bf16[512,256]{0,1:T(8,128)(2,1)S(1)}, bf16[512,256]{0,1:T(8,128)(2,1)}, u32[]{:S(2)}) copy-start(bf16[512,256]{0,1:T(8,128)(2,1)} %fusion.7) | copy-start | bytes 786436
  178.2 156.0 %all-gather.17.cloned.1.call-start = ((), (), s32[]{:S(2)}) async-start(), calls=%async_computation.5 | async-start | bytes 2359296 | tf_op jit(solution)/shard_map/all_gather | solution.py:30
Sparse Core Ops, SparseCore 0:
  9.7 54.5 all-gather.8
  65.9 46.5 all-gather.6
  117.5 55.2 all-gather.10
  177.8 56.2 all-gather.14
  235.6 38.7 all-gather.12
  279.3 54.8 all-gather.16
where the time goes:
time: 349 us; the launch traced here: 346 us
  waiting for transfers between devices  312 us (89%)
  matrix products  18.6 us (5%)
  between operations  13.5 us (4%)
    all_gather x2, waiting for transfers between devices, shards(): columns = lax.all_gather(current, 'row', axis=0, tiled=True)  111 us
    all_gather x2, waiting for transfers between devices, shards(): lax.all_gather(square, 'row', axis=0, tiled=True)  110 us
    all_gather x2, waiting for transfers between devices, shards(): left_part = lax.all_gather(current, 'col', axis=1, tiled=True)  88.6 us
    dot_general x4, matrix products, contract(): return jnp.dot(left_part, right_part, preferred_element_type=jnp.float32)  18.6 us
  transfers between devices with their start and end apart: 6, of which 6 were waited for; matrix products, arithmetic and copies ran while one was open for 0% of the time, Pallas kernels for 0%

commit v1 on v0

v1 whole, which is shorter than its diff:
```python
import jax
import jax.numpy as jnp
from jax import lax
from jax.experimental import pallas as pl
from jax.experimental.pallas import tpu as pltpu
from jax.sharding import PartitionSpec as P

MESH = pl.DeviceIdType.MESH
BLOCK = 128
ROWS, COLS = 512, 256
HALF = ROWS // 2
RING = 4


class Gather:
    def __init__(self, buf, place, device, ring, plane, send, recv):
        self.buf, self.place, self.device = buf, place, device
        self.ring, self.plane = ring, plane
        self.send, self.recv = send, recv

    def copy(self, i):
        half, side, plane, hops = {
            0: (0, 1, 0, 0), 1: (1, 1, 0, 0), 2: (0, -1, 0, 0), 3: (1, -1, 0, 0), 4: (0, 0, 0, 0), 5: (1, 0, 0, 0),
            6: (0, 1, 0, 1), 7: (1, -1, 0, 1),
            8: (0, 1, 1, 0), 9: (1, 1, 1, 0), 10: (0, -1, 1, 0), 11: (1, -1, 1, 0),
            12: (0, 1, 1, 1), 13: (1, -1, 1, 1),
        }[i]
        me, p = self.ring, self.plane
        whose = (lax.rem(me - side * hops + RING, RING), p if plane == 0 else 1 - p)
        target = (lax.rem(me + side + RING, RING), p if side else 1 - p)
        ref = self.buf.at[self.place(*whose), pl.ds(half * HALF, HALF)]
        return pltpu.make_async_remote_copy(
            src_ref=ref, dst_ref=ref, send_sem=self.send.at[i], recv_sem=self.recv.at[i],
            device_id=self.device(*target), device_id_type=MESH,
        )

    def arrived(self, i):
        self.copy(i).wait_recv()

    def own(self):
        for i in (0, 3, 4, 2, 1, 5):
            self.copy(i).start()

    def sent(self):
        for i in range(14):
            self.copy(i).wait_send()


STEPS = (((0,), (6,)), ((3,), (7,)), ((4,), (8, 10)), ((5,), (11, 9)), ((8,), (12,)), ((11,), (13,)))
REST = (1, 2, 6, 7, 9, 10, 12, 13)
WHOLE = {1: (-1, 0), 2: (1, 0), 5: (0, 1), 7: (2, 0), 9: (-1, 1), 10: (1, 1), 13: (2, 1)}


def kernel(pattern_ref, y_ref, out_ref, rows, cols, squares, total, send, recv, pair_send, pair_recv):
    row = lax.axis_index("row")
    col = lax.axis_index("col")
    x, z_hi = lax.rem(row, 4), row // 4
    y, z_lo, core = col // 4, lax.rem(col // 2, 2), lax.rem(col, 2)

    def in_row(y_, z_):
        return row, y_ * 4 + z_ * 2 + core

    def in_col(x_, z_):
        return z_ * 4 + x_, col

    sibling = (row, col + 1 - 2 * core)
    barrier = pltpu.get_barrier_semaphore()
    partners = [sibling, in_row(y, 1 - z_lo), in_col(x, 1 - z_hi)]
    for side in (1, 3):
        partners += [in_row(lax.rem(y + side, 4), z_lo), in_col(lax.rem(x + side, 4), z_hi)]
    for partner in partners:
        pl.semaphore_signal(barrier, inc=1, device_id=partner, device_id_type=MESH)
    rows[0, col] = y_ref[...]
    cols[0, row] = y_ref[...]
    pl.semaphore_wait(barrier, len(partners))

    def masked(blocks, store):
        for i in range(ROWS // BLOCK):
            for j in range(COLS // BLOCK):
                keep = pattern_ref[row * 4 + i, col * 2 + j].astype(jnp.float32)
                at = (pl.ds(i * BLOCK, BLOCK), pl.ds(j * BLOCK, BLOCK))
                store(at, keep * blocks(at))

    def product(left, right):
        total[...] = jnp.zeros_like(total)

        def body(k, _):
            part = jnp.dot(left[2 * k], right[k, 0:COLS], preferred_element_type=jnp.float32)
            part += jnp.dot(left[2 * k + 1], right[k, COLS : 2 * COLS], preferred_element_type=jnp.float32)
            total[...] += part
            return 0

        lax.fori_loop(0, 8, body, 0)

    for step in range(2):
        y_rows, y_cols, square = rows.at[step], cols.at[step], squares.at[step]
        by_row = Gather(y_rows, lambda y_, z_: y_ * 4 + z_ * 2 + core, in_row, y, z_lo, send.at[3 * step], recv.at[3 * step])
        by_col = Gather(y_cols, lambda x_, z_: z_ * 4 + x_, in_col, x, z_hi, send.at[3 * step + 1], recv.at[3 * step + 1])

        def share(n, y_, z_):
            ref = y_rows.at[y_ * 4 + z_ * 2 + core]
            return pltpu.make_async_remote_copy(
                src_ref=ref, dst_ref=ref, send_sem=pair_send.at[step, n], recv_sem=pair_recv.at[step, n],
                device_id=sibling, device_id_type=MESH,
            )

        shares = [share(0, y, z_lo)]
        by_row.own()
        by_col.own()
        shares[0].start()
        for waits, starts in STEPS:
            for g in (by_row, by_col):
                for i in waits:
                    g.arrived(i)
                for i in starts:
                    g.copy(i).start()
            if waits == (5,):
                shares.append(share(1, y, 1 - z_lo))
                shares[-1].start()
        for i in REST:
            by_row.arrived(i)
            by_col.arrived(i)
            if i in WHOLE:
                offset, other = WHOLE[i]
                shares.append(share(len(shares), lax.rem(y + offset + 4, 4), 1 - z_lo if other else z_lo))
                shares[-1].start()
        for s in shares:
            s.wait_recv()
        product(y_rows, y_cols)
        scale = 1.0 / (3.0 * 4096)

        def store_square(at, value):
            square[row, at[0], at[1]] = value.astype(jnp.bfloat16)

        masked(lambda at: total[at] * scale, store_square)
        by_square = Gather(square, lambda x_, z_: z_ * 4 + x_, in_col, x, z_hi, send.at[3 * step + 2], recv.at[3 * step + 2])
        by_square.own()
        for waits, starts in STEPS:
            for i in waits:
                by_square.arrived(i)
            for i in starts:
                by_square.copy(i).start()
        for i in REST:
            by_square.arrived(i)
        product(y_rows, square)

        def updated(at):
            return 1.5 * y_rows[col, at[0], at[1]].astype(jnp.float32) - 0.5 * total[at]

        if step == 0:
            def store_next(at, value):
                rows[1, col, at[0], at[1]] = value.astype(jnp.bfloat16)
                cols[1, row, at[0], at[1]] = value.astype(jnp.bfloat16)

            masked(updated, store_next)
        else:
            def store_out(at, value):
                out_ref[at] = value

            masked(updated, store_out)
        by_row.sent()
        by_col.sent()
        by_square.sent()
        for s in shares:
            s.wait_send()


def shards(pattern, matrix):
    return pl.pallas_call(
        kernel,
        name="sign_steps",
        out_shape=jax.ShapeDtypeStruct((ROWS, COLS), jnp.float32),
        in_specs=[pl.BlockSpec(memory_space=pltpu.SMEM), pl.BlockSpec(memory_space=pltpu.VMEM)],
        out_specs=pl.BlockSpec(memory_space=pltpu.VMEM),
        scratch_shapes=[
            pltpu.VMEM((2, 16, ROWS, COLS), jnp.bfloat16),
            pltpu.VMEM((2, 8, ROWS, COLS), jnp.bfloat16),
            pltpu.VMEM((2, 8, ROWS, COLS), jnp.bfloat16),
            pltpu.VMEM((ROWS, COLS), jnp.float32),
            pltpu.SemaphoreType.DMA((6, 14)),
            pltpu.SemaphoreType.DMA((6, 14)),
            pltpu.SemaphoreType.DMA((2, 8)),
            pltpu.SemaphoreType.DMA((2, 8)),
        ],
        compiler_params=pltpu.CompilerParams(collective_id=0, has_side_effects=True, vmem_limit_bytes=40 << 20),
        cost_estimate=pl.CostEstimate(flops=4 * 2 * 512 * 256 * 4096, bytes_accessed=1 << 20, transcendentals=0),
    )(pattern, matrix)


def solution(mesh):
    in_specs = (P(), P("row", "col"))
    return jax.shard_map(shards, mesh=mesh, in_specs=in_specs, out_specs=P("row", "col"), check_vma=False)
```

time: 349 us -> 108 us (0.31)
  waiting for transfers between devices: 312 us -> 0 us
  Pallas kernels: 0 us -> 105 us
  matrix products: 18.6 us -> 0 us
  between operations: 13.5 us -> 0.01 us
    all_gather x6 -> x0, waiting for transfers between devices: 310 us -> none  [the longest x2 111 us: shards(): columns = lax.all_gather(current, 'row', axis=0, tiled=True)]
    pallas_call x0 -> x1, Pallas kernels: none -> 105 us  [shards(): pl.pallas_call(kernel, name='sign_steps', out_shape=jax.ShapeDtypeStruct(...]
    dot_general x4 -> x0, matrix products: 18.6 us -> none  [contract(): return jnp.dot(left_part, right_part, preferred_element_type=jnp.float32)]
  transfers between devices with their start and end apart: 6 -> 0, of which waited for: 6 -> 0; matrix products, arithmetic and copies ran while one was open for 0% -> 0% of each run, Pallas kernels for 0% -> 0%
where the time goes in v1:
time: 108 us
  Pallas kernels  105 us (97%)
  local copies, waits for them, and re-layouts  2.46 us (2%)
    pallas_call x1, Pallas kernels, shards(): pl.pallas_call(kernel, name='sign_steps', out_shape=jax.ShapeDtypeStruct(...  105 us
    unnamed x5, local copies, waits for them, and re-layouts  2.46 us

profile of v1, /device:TPU:5, one launch (start us, length us, event | category | flops | bytes accessed | tf_op | source)
XLA Modules:
  0.0 107.5 jit_solution(1397625811896074583)
XLA Ops:
  0.0 0.0 copy-start
  0.0 0.9 copy-done
  1.0 0.0 copy-start.1
  1.0 0.7 copy-done.1
  1.7 105.1 %sign_steps.1 = f32[512,256]{1,0:T(8,128)S(1)} custom-call(s32[32,32]{1,0:T(8,128)S(1)} %copy-done.1, bf16[512,256]{1,0:T(8,128)(2,1)S(1)} %copy-done), custom_call_target="tpu_custom_call" | custom-call | flops 4294967296 | bytes 1048576 | tf_op jit(solution)/shard_map/sign_steps/pallas_call | solution.py:169
  106.7 0.8 copy.4
Async XLA Ops:
  0.0 0.9 copy-start
  1.0 0.7 copy-start.1

commit v2 on v0

v2 whole, which is shorter than its diff:
```python
import jax
import jax.numpy as jnp
from jax import lax
from jax.experimental import pallas as pl
from jax.experimental.pallas import tpu as pltpu
from jax.sharding import PartitionSpec as P

MESH = pl.DeviceIdType.MESH
BLOCK = 128
ROWS, COLS = 512, 256
RING = 4
F32 = jnp.float32

COPIES = (
    (0, 1, 0, 0), (1, 1, 0, 0), (0, -1, 0, 0), (1, -1, 0, 0), (0, 0, 0, 0), (1, 0, 0, 0),
    (0, 1, 0, 1), (1, -1, 0, 1),
    (0, 1, 1, 0), (1, 1, 1, 0), (0, -1, 1, 0), (1, -1, 1, 0),
    (0, 1, 1, 1), (1, -1, 1, 1),
)
OWN = (0, 3, 4, 5, 2, 1)
RELAYS = ((0, (6,)), (3, (7,)), (4, (8, 10)), (5, (11, 9)), (8, (12,)), (11, (13,)))
NEAR = (1, 2, 6, 7)
FAR = (9, 10, 12, 13)
WHOLE = {5: (0, 1), 1: (-1, 0), 2: (1, 0), 7: (2, 0), 9: (-1, 1), 10: (1, 1), 13: (2, 1)}


def ring(i):
    return lax.rem(i + RING, RING)


def reach(cell, other):
    dx = lax.max(cell[0] - other[0], other[0] - cell[0])
    dy = lax.max(cell[1] - other[1], other[1] - cell[1])
    return jnp.where(dy == 3, -1, lax.min(2, 3 - dx - dy))


def run(width, inner, core):
    if not inner:
        return core * (3 - width), width + 1
    return ((core + 1, 1), (core, 3), (0, 4))[width]


def when_reach(r, action):
    for width in range(3):
        pl.when(r == width)(lambda width=width: action(width))


class Gather:
    def __init__(self, buf, place, device, cell, fixed, core, me, plane, send, recv):
        self.buf, self.place, self.device, self.cell = buf, place, device, cell
        self.fixed, self.core, self.me, self.plane = fixed, core, me, plane
        self.send, self.recv = send, recv

    def each(self, i, arriving, action):
        inner, side, other, hops = COPIES[i]
        if side:
            owner = (ring(self.me - side * (hops + arriving)), 1 - self.plane if other else self.plane)
        else:
            owner = (self.me, 1 - self.plane if arriving else self.plane)
        target = (ring(self.me + side), self.plane if side else 1 - self.plane)
        j = 1 - self.core if inner else self.core

        def act(width):
            low, count = run(width, inner, self.core)
            ref = self.buf.at[self.place(*owner), j, pl.ds(low * BLOCK, count * BLOCK)]
            action(pltpu.make_async_remote_copy(
                src_ref=ref, dst_ref=ref, send_sem=self.send.at[i], recv_sem=self.recv.at[i],
                device_id=self.device(*target), device_id_type=MESH,
            ))

        when_reach(reach(self.cell(*owner), self.fixed), act)

    def start(self, *numbers):
        for i in numbers:
            self.each(i, 0, lambda copy: copy.start())

    def arrived(self, i):
        self.each(i, 1, lambda copy: copy.wait_recv())

    def sent(self):
        for i in range(len(COPIES)):
            self.each(i, 0, lambda copy: copy.wait_send())


def kernel(pattern_hbm, y_hbm, out_ref, pattern, rows, cols, squares, total, local, send, recv, pair_send, pair_recv):
    row = lax.axis_index("row")
    col = lax.axis_index("col")
    x, z_hi = lax.rem(row, 4), row // 4
    y, z_lo, core = col // 4, lax.rem(col // 2, 2), lax.rem(col, 2)

    def in_row(y_, z_):
        return row, y_ * 4 + z_ * 2 + core

    def in_col(x_, z_):
        return z_ * 4 + x_, col

    def row_place(y_, z_):
        return y_ * 4 + z_ * 2 + core

    def col_place(x_, z_):
        return z_ * 4 + x_

    def row_cell(y_, z_):
        return y_ // 2, lax.rem(y_, 2) * 2 + z_

    def col_cell(x_, z_):
        return z_, x_

    p, q = col_cell(x, z_hi), row_cell(y, z_lo)
    sibling = (row, col + 1 - 2 * core)
    barrier = pltpu.get_barrier_semaphore()
    partners = [sibling, in_row(y, 1 - z_lo), in_col(x, 1 - z_hi)]
    for side in (1, 3):
        partners += [in_row(ring(y + side), z_lo), in_col(ring(x + side), z_hi)]
    for partner in partners:
        pl.semaphore_signal(barrier, inc=1, device_id=partner, device_id_type=MESH)
    loads = [pltpu.make_async_copy(pattern_hbm, pattern, local.at[4])]
    for j in range(2):
        half = y_hbm.at[:, pl.ds(j * BLOCK, BLOCK)]
        loads.append(pltpu.make_async_copy(half, rows.at[0, col, j], local.at[j]))
        loads.append(pltpu.make_async_copy(half, cols.at[0, row, j], local.at[2 + j]))
    for load in loads:
        load.start()
    for load in loads:
        load.wait()
    pl.semaphore_wait(barrier, len(partners))

    def clear(refs, place, cell, fixed, side):
        def wipe(j, low, count):
            for ref in refs:
                for step in range(2):
                    ref[step, place, j, pl.ds(low * BLOCK, count * BLOCK)] = jnp.zeros((count * BLOCK, BLOCK), jnp.bfloat16)

        r = reach(cell, fixed)

        @pl.when(r == -1)
        def _():
            for j in range(2):
                wipe(j, 0, 4)

        def act(width):
            wipe(side, (1 - side) * (width + 1), 3 - width)
            if width == 1:
                wipe(1 - side, (1 - side) * 3, 1)
            if width == 0:
                for low in (0, 2 - side, 3):
                    wipe(1 - side, low, 1)

        when_reach(r, act)

    def clear_all():
        def at_row(s, _):
            clear((rows,), s, row_cell(s // 4, lax.rem(s // 2, 2)), p, lax.rem(s, 2))
            return 0

        def at_col(s, _):
            clear((cols, squares), s, col_cell(lax.rem(s, 4), s // 4), q, core)
            return 0

        lax.fori_loop(0, 16, at_row, 0)
        lax.fori_loop(0, 8, at_col, 0)

    def product(left, right, m, places):
        at = pl.ds(m * COLS, COLS)
        terms = []
        for k in places:
            for c in range(2):
                l = jnp.concatenate([left[2 * k + c, j, at] for j in range(2)], axis=1)
                r = jnp.concatenate([right[k, j, pl.ds(c * COLS, COLS)] for j in range(2)], axis=1)
                terms.append(jnp.dot(l, r, preferred_element_type=F32))
        return sum(terms)

    def masked(m, value, store):
        for i in range(2):
            for j in range(2):
                keep = pattern[row * 4 + 2 * m + i, col * 2 + j].astype(F32)
                block = value(pl.ds((2 * m + i) * BLOCK, BLOCK), i, j)
                store(pl.ds((2 * m + i) * BLOCK, BLOCK), j, keep * block)

    def one_step(step, _):
        y_rows, y_cols, square = rows.at[step], cols.at[step], squares.at[step]
        n = 3 * step
        by_row = Gather(y_rows, row_place, in_row, row_cell, p, core, y, z_lo, send.at[n], recv.at[n])
        by_col = Gather(y_cols, col_place, in_col, col_cell, q, core, x, z_hi, send.at[n + 1], recv.at[n + 1])
        by_square = Gather(square, col_place, in_col, col_cell, q, core, x, z_hi, send.at[n + 2], recv.at[n + 2])
        shared = []

        def share(number, y_, z_, side, action):
            whose = 1 - core if side else core

            def act(width):
                for inner in range(2):
                    low, count = run(width, inner, whose)
                    j = 1 - whose if inner else whose
                    ref = y_rows.at[y_ * 4 + z_ * 2 + whose, j, pl.ds(low * BLOCK, count * BLOCK)]
                    action(pltpu.make_async_remote_copy(
                        src_ref=ref, dst_ref=ref, send_sem=pair_send.at[step, number, inner],
                        recv_sem=pair_recv.at[step, number, inner], device_id=sibling, device_id_type=MESH,
                    ))

            when_reach(reach(row_cell(y_, z_), p), act)

        def share_start(y_, z_):
            share(len(shared), y_, z_, 0, lambda copy: copy.start())
            shared.append((y_, z_))

        by_row.start(*OWN)
        by_col.start(*OWN)
        share_start(y, z_lo)
        pl.when(step == 0)(clear_all)
        for i, then in RELAYS:
            for g in (by_row, by_col):
                g.arrived(i)
                g.start(*then)
            if i in WHOLE:
                share_start(y, 1 - z_lo)
        for i in NEAR + FAR:
            by_row.arrived(i)
            if i in WHOLE:
                offset, other = WHOLE[i]
                share_start(ring(y + offset), 1 - z_lo if other else z_lo)
        for i in NEAR + FAR:
            by_col.arrived(i)
        for number, (y_, z_) in enumerate(shared):
            share(number, y_, z_, 1, lambda copy: copy.wait_recv())
        scale = 1.0 / (3.0 * 4096)
        for m in range(2):
            full = product(y_rows, y_cols, m, range(8))

            def store_square(at, j, block):
                square[row, j, at] = block.astype(jnp.bfloat16)

            masked(m, lambda at, i, j: full[i * BLOCK : (i + 1) * BLOCK, j * BLOCK : (j + 1) * BLOCK] * scale, store_square)
        by_square.start(*OWN)
        for i, then in RELAYS:
            by_square.arrived(i)
            by_square.start(*then)
        for i in NEAR:
            by_square.arrived(i)
        for m in range(2):
            total[pl.ds(m * COLS, COLS)] = product(y_rows, square, m, [z_hi * 4 + k for k in range(4)])
        for i in FAR:
            by_square.arrived(i)
        for m in range(2):
            full = total[pl.ds(m * COLS, COLS)] + product(y_rows, square, m, [(1 - z_hi) * 4 + k for k in range(4)])

            def updated(at, i, j):
                cube = full[i * BLOCK : (i + 1) * BLOCK, j * BLOCK : (j + 1) * BLOCK]
                return 1.5 * y_rows[col, j, at].astype(F32) - 0.5 * cube

            def store_next(at, j, block):
                @pl.when(step == 0)
                def _():
                    rows[1, col, j, at] = block.astype(jnp.bfloat16)
                    cols[1, row, j, at] = block.astype(jnp.bfloat16)

                @pl.when(step == 1)
                def _():
                    out_ref[at, pl.ds(j * BLOCK, BLOCK)] = block

            masked(m, updated, store_next)
        for g in (by_row, by_col, by_square):
            g.sent()
        for number, (y_, z_) in enumerate(shared):
            share(number, y_, z_, 0, lambda copy: copy.wait_send())
        return 0

    lax.fori_loop(0, 2, one_step, 0)


def shards(pattern, matrix):
    return pl.pallas_call(
        kernel,
        name="sign_steps",
        out_shape=jax.ShapeDtypeStruct((ROWS, COLS), F32),
        in_specs=[pl.BlockSpec(memory_space=pl.ANY), pl.BlockSpec(memory_space=pl.ANY)],
        out_specs=pl.BlockSpec(memory_space=pltpu.VMEM),
        scratch_shapes=[
            pltpu.SMEM((32, 32), jnp.int32),
            pltpu.VMEM((2, 16, 2, ROWS, BLOCK), jnp.bfloat16),
            pltpu.VMEM((2, 8, 2, ROWS, BLOCK), jnp.bfloat16),
            pltpu.VMEM((2, 8, 2, ROWS, BLOCK), jnp.bfloat16),
            pltpu.VMEM((ROWS, COLS), F32),
            pltpu.SemaphoreType.DMA((5,)),
            pltpu.SemaphoreType.DMA((6, len(COPIES))),
            pltpu.SemaphoreType.DMA((6, len(COPIES))),
            pltpu.SemaphoreType.DMA((2, 8, 2)),
            pltpu.SemaphoreType.DMA((2, 8, 2)),
        ],
        compiler_params=pltpu.CompilerParams(collective_id=0, has_side_effects=True, vmem_limit_bytes=56 << 20),
        cost_estimate=pl.CostEstimate(flops=4 * 2 * 512 * 256 * 4096, bytes_accessed=1 << 20, transcendentals=0),
    )(pattern, matrix)


def solution(mesh):
    in_specs = (P(), P("row", "col"))
    return jax.shard_map(shards, mesh=mesh, in_specs=in_specs, out_specs=P("row", "col"), check_vma=False)
```

time: 349 us -> 92.1 us (0.26)
  waiting for transfers between devices: 312 us -> 0 us
  Pallas kernels: 0 us -> 90 us
  matrix products: 18.6 us -> 0 us
  between operations: 13.5 us -> 0.01 us
    all_gather x6 -> x0, waiting for transfers between devices: 310 us -> none  [the longest x2 111 us: shards(): columns = lax.all_gather(current, 'row', axis=0, tiled=True)]
    pallas_call x0 -> x1, Pallas kernels: none -> 90 us  [shards(): pl.pallas_call(kernel, name='sign_steps', out_shape=jax.ShapeDtypeStruct(...]
    dot_general x4 -> x0, matrix products: 18.6 us -> none  [contract(): return jnp.dot(left_part, right_part, preferred_element_type=jnp.float32)]
  transfers between devices with their start and end apart: 6 -> 0, of which waited for: 6 -> 0; matrix products, arithmetic and copies ran while one was open for 0% -> 0% of each run, Pallas kernels for 0% -> 0%
where the time goes in v2:
time: 92.1 us; the launch traced here: 91.9 us
  Pallas kernels  90 us (98%)
  local copies, waits for them, and re-layouts  1.87 us (2%)
    pallas_call x1, Pallas kernels, shards(): pl.pallas_call(kernel, name='sign_steps', out_shape=jax.ShapeDtypeStruct(...  90 us
    unnamed x1, local copies, waits for them, and re-layouts  1.87 us

profile of v2, /device:TPU:5, one launch (start us, length us, event | category | flops | bytes accessed | tf_op | source)
XLA Modules:
  0.0 91.9 jit_solution(17742510527963081600)
XLA Ops:
  0.0 90.0 %sign_steps.1 = f32[512,256]{1,0:T(8,128)} custom-call(s32[32,32]{1,0:T(8,128)} %pattern_hbm.1, bf16[512,256]{1,0:T(8,128)(2,1)} %y_hbm.1), custom_call_target="tpu_custom_call" | custom-call | flops 4294967296 | bytes 1048576 | tf_op jit(solution)/shard_map/sign_steps/pallas_call | solution.py:272
  90.0 1.9 %copy.4 = f32[512,256]{1,0:T(8,128)} copy(f32[512,256]{1,0:T(8,128)} %sign_steps.1) | data formatting | bytes 1048576

commit v3 on v2

--- a/solution.py
+++ b/solution.py
@@ -12,16 +12,37 @@
 F32 = jnp.float32
 
 COPIES = (
-    (0, 1, 0, 0), (1, 1, 0, 0), (0, -1, 0, 0), (1, -1, 0, 0), (0, 0, 0, 0), (1, 0, 0, 0),
-    (0, 1, 0, 1), (1, -1, 0, 1),
-    (0, 1, 1, 0), (1, 1, 1, 0), (0, -1, 1, 0), (1, -1, 1, 0),
-    (0, 1, 1, 1), (1, -1, 1, 1),
+    ("up", 1, 0, 0), ("not up", 1, 0, 0), ("not down", -1, 0, 0), ("down", -1, 0, 0), ("up", 0, 0, 0), ("not up", 0, 0, 0),
+    ("relay", 1, -1, 0), ("relay down", -1, 1, 0),
+    ("up", 1, 0, 1), ("not up", 1, 0, 1), ("not down", -1, 0, 1), ("down", -1, 0, 1),
+    ("relay", 1, -1, 1), ("relay down", -1, 1, 1),
 )
-OWN = (0, 3, 4, 5, 2, 1)
-RELAYS = ((0, (6,)), (3, (7,)), (4, (8, 10)), (5, (11, 9)), (8, (12,)), (11, (13,)))
-NEAR = (1, 2, 6, 7)
-FAR = (9, 10, 12, 13)
-WHOLE = {5: (0, 1), 1: (-1, 0), 2: (1, 0), 7: (2, 0), 9: (-1, 1), 10: (1, 1), 13: (2, 1)}
+ACROSS = COPIES[:12] + (("far", 0, 2, 0), ("not far", 0, 2, 0))
+SECOND = (1, 2, 9, 10)
+
+
+def same_halves(me, half):
+    return half in ("up", "not down", "relay", "far")
+
+
+def near_centre(me, half):
+    return {
+        "up": me < 2, "not up": me >= 2, "down": me >= 2, "not down": me < 2, "relay": (me + 1) // 2 == 1,
+        "relay down": (me + 1) // 2 == 1, "far": me >= 2, "not far": me < 2,
+    }[half]
+
+
+AROUND = (COPIES, {0: (6,), 3: (7,), 4: (8,), 5: (11, 9, 10), 8: (12,), 11: (13,)})
+OVER = (ACROSS, {0: (6,), 3: (7,), 4: (8, 10), 5: (11, 9), 6: (12,), 7: (13,)})
+TILES = {(0, 1): (-1, 0), (2, 3): (1, 0), (4, 5): (0, 1), (6, 7): (2, 0), (8, 9): (-1, 1), (10, 11): (1, 1), (12, 13): (2, 1)}
+OWN = ("c4", "c0", "r0", "c3", "r3", "c5", "c1", "r1", "c2", "r2", "r4", "r5")
+WAITS = (
+    "r0", "c0", "r3", "c3", "c4", "c5", "r1", "r2", "r6", "r7", "r4", "c8", "c11", "r5",
+    "r8", "r9", "r10", "r11", "r12", "r13", "c1", "c2", "c6", "c7", "c9", "c10", "c12", "c13",
+)
+SQUARE_OWN = (4, 0, 3, 5, 1, 2)
+SQUARE_WAITS = (0, 3, 4, 5, 6, 7, 1, 2, 8, 9, 10, 11, 12, 13)
+ROW_KIND, COL_KIND, SQUARE_KIND = OVER, AROUND, OVER
 
 
 def ring(i):
@@ -46,29 +67,40 @@
 
 
 class Gather:
-    def __init__(self, buf, place, device, cell, fixed, core, me, plane, send, recv):
+    def __init__(self, buf, place, device, cell, fixed, core, me, plane, send, recv, kind, halves):
+        self.copies, self.then = kind
+        self.halves = halves
         self.buf, self.place, self.device, self.cell = buf, place, device, cell
         self.fixed, self.core, self.me, self.plane = fixed, core, me, plane
         self.send, self.recv = send, recv
 
     def each(self, i, arriving, action):
-        inner, side, other, hops = COPIES[i]
-        if side:
-            owner = (ring(self.me - side * (hops + arriving)), 1 - self.plane if other else self.plane)
-        else:
-            owner = (self.me, 1 - self.plane if arriving else self.plane)
+        half, side, offset, other = self.copies[i]
+        sender = ring(self.me - side) if arriving and side else self.me
+        plane = 1 - self.plane if arriving and not side else self.plane
+        owner = (ring(sender + offset), 1 - plane if other else plane)
         target = (ring(self.me + side), self.plane if side else 1 - self.plane)
-        j = 1 - self.core if inner else self.core
-
-        def act(width):
+        outer = self.halves(sender, half)
+        r = reach(self.cell(*owner), self.fixed)
+        if self.halves is near_centre and i in SECOND:
+            r = jnp.where(sender == (3 if side > 0 else 0), -1, r)
+
+        def act(width, inner):
             low, count = run(width, inner, self.core)
+            j = 1 - self.core if inner else self.core
             ref = self.buf.at[self.place(*owner), j, pl.ds(low * BLOCK, count * BLOCK)]
             action(pltpu.make_async_remote_copy(
                 src_ref=ref, dst_ref=ref, send_sem=self.send.at[i], recv_sem=self.recv.at[i],
                 device_id=self.device(*target), device_id_type=MESH,
             ))
 
-        when_reach(reach(self.cell(*owner), self.fixed), act)
+        if isinstance(outer, bool):
+            when_reach(r, lambda width: act(width, not outer))
+        else:
+            code = r * 2 + jnp.where(outer, 0, 1)
+            for width in range(3):
+                for inner in (False, True):
+                    pl.when(code == 2 * width + inner)(lambda width=width, inner=inner: act(width, inner))
 
     def start(self, *numbers):
         for i in numbers:
@@ -76,6 +108,7 @@
 
     def arrived(self, i):
         self.each(i, 1, lambda copy: copy.wait_recv())
+        self.start(*self.then.get(i, ()))
 
     def sent(self):
         for i in range(len(COPIES)):
@@ -147,17 +180,19 @@
                     wipe(1 - side, low, 1)
 
         when_reach(r, act)
+        return wipe
 
     def clear_all():
         def at_row(s, _):
-            clear((rows,), s, row_cell(s // 4, lax.rem(s // 2, 2)), p, lax.rem(s, 2))
+            clear((rows,), 2 * s + core, row_cell(s // 2, lax.rem(s, 2)), p, core)
             return 0
 
         def at_col(s, _):
-            clear((cols, squares), s, col_cell(lax.rem(s, 4), s // 4), q, core)
+            wipe = clear((cols, squares), s, col_cell(lax.rem(s, 4), s // 4), q, core)
+            pl.when(lax.rem(s, 4) + x == 3)(lambda: pl.when(lax.rem(x, 3) == 0)(lambda: wipe(core, 0, 4)))
             return 0
 
-        lax.fori_loop(0, 16, at_row, 0)
+        lax.fori_loop(0, 8, at_row, 0)
         lax.fori_loop(0, 8, at_col, 0)
 
     def product(left, right, m, places):
@@ -177,52 +212,45 @@
                 block = value(pl.ds((2 * m + i) * BLOCK, BLOCK), i, j)
                 store(pl.ds((2 * m + i) * BLOCK, BLOCK), j, keep * block)
 
+    def square_gather(step):
+        n = 3 * step + 2
+        return Gather(squares.at[step], col_place, in_col, col_cell, q, core, x, z_hi, send.at[n], recv.at[n], SQUARE_KIND, near_centre)
+
     def one_step(step, _):
         y_rows, y_cols, square = rows.at[step], cols.at[step], squares.at[step]
         n = 3 * step
-        by_row = Gather(y_rows, row_place, in_row, row_cell, p, core, y, z_lo, send.at[n], recv.at[n])
-        by_col = Gather(y_cols, col_place, in_col, col_cell, q, core, x, z_hi, send.at[n + 1], recv.at[n + 1])
-        by_square = Gather(square, col_place, in_col, col_cell, q, core, x, z_hi, send.at[n + 2], recv.at[n + 2])
+        by_row = Gather(y_rows, row_place, in_row, row_cell, p, core, y, z_lo, send.at[n], recv.at[n], ROW_KIND, same_halves)
+        by_col = Gather(y_cols, col_place, in_col, col_cell, q, core, x, z_hi, send.at[n + 1], recv.at[n + 1], COL_KIND, near_centre)
+        by_square = square_gather(step)
         shared = []
 
-        def share(number, y_, z_, side, action):
-            whose = 1 - core if side else core
-
-            def act(width):
-                for inner in range(2):
-                    low, count = run(width, inner, whose)
-                    j = 1 - whose if inner else whose
-                    ref = y_rows.at[y_ * 4 + z_ * 2 + whose, j, pl.ds(low * BLOCK, count * BLOCK)]
-                    action(pltpu.make_async_remote_copy(
-                        src_ref=ref, dst_ref=ref, send_sem=pair_send.at[step, number, inner],
-                        recv_sem=pair_recv.at[step, number, inner], device_id=sibling, device_id_type=MESH,
-                    ))
-
-            when_reach(reach(row_cell(y_, z_), p), act)
+        def share(number, y_, z_, side):
+            ref = y_rows.at[y_ * 4 + z_ * 2 + (1 - core if side else core)]
+            return pltpu.make_async_remote_copy(
+                src_ref=ref, dst_ref=ref, send_sem=pair_send.at[step, number], recv_sem=pair_recv.at[step, number],
+                device_id=sibling, device_id_type=MESH,
+            )
 
         def share_start(y_, z_):
-            share(len(shared), y_, z_, 0, lambda copy: copy.start())
+            share(len(shared), y_, z_, 0).start()
             shared.append((y_, z_))
 
-        by_row.start(*OWN)
-        by_col.start(*OWN)
+        gathers = {"r": by_row, "c": by_col}
+        for name in OWN:
+            gathers[name[0]].start(int(name[1:]))
+        pl.when(step == 0)(clear_all)
         share_start(y, z_lo)
-        pl.when(step == 0)(clear_all)
-        for i, then in RELAYS:
-            for g in (by_row, by_col):
-                g.arrived(i)
-                g.start(*then)
-            if i in WHOLE:
-                share_start(y, 1 - z_lo)
-        for i in NEAR + FAR:
-            by_row.arrived(i)
-            if i in WHOLE:
-                offset, other = WHOLE[i]
-                share_start(ring(y + offset), 1 - z_lo if other else z_lo)
-        for i in NEAR + FAR:
-            by_col.arrived(i)
+        here = set()
+        for name in WAITS:
+            gathers[name[0]].arrived(int(name[1:]))
+            if name[0] == "r":
+                here.add(int(name[1:]))
+                for parts, (offset, other) in TILES.items():
+                    if int(name[1:]) in parts and here.issuperset(parts):
+                        share_start(ring(y + offset), 1 - z_lo if other else z_lo)
+        pl.when(step == 1)(square_gather(0).sent)
         for number, (y_, z_) in enumerate(shared):
-            share(number, y_, z_, 1, lambda copy: copy.wait_recv())
+            share(number, y_, z_, 1).wait_recv()
         scale = 1.0 / (3.0 * 4096)
         for m in range(2):
             full = product(y_rows, y_cols, m, range(8))
@@ -231,15 +259,16 @@
                 square[row, j, at] = block.astype(jnp.bfloat16)
 
             masked(m, lambda at, i, j: full[i * BLOCK : (i + 1) * BLOCK, j * BLOCK : (j + 1) * BLOCK] * scale, store_square)
-        by_square.start(*OWN)
-        for i, then in RELAYS:
+        by_square.start(*SQUARE_OWN)
+        for i in SQUARE_WAITS[:8]:
             by_square.arrived(i)
-            by_square.start(*then)
-        for i in NEAR:
-            by_square.arrived(i)
+        by_row.sent()
+        by_col.sent()
+        for number, (y_, z_) in enumerate(shared):
+            share(number, y_, z_, 0).wait_send()
         for m in range(2):
             total[pl.ds(m * COLS, COLS)] = product(y_rows, square, m, [z_hi * 4 + k for k in range(4)])
-        for i in FAR:
+        for i in SQUARE_WAITS[8:]:
             by_square.arrived(i)
         for m in range(2):
             full = total[pl.ds(m * COLS, COLS)] + product(y_rows, square, m, [(1 - z_hi) * 4 + k for k in range(4)])
@@ -259,13 +288,10 @@
                     out_ref[at, pl.ds(j * BLOCK, BLOCK)] = block
 
             masked(m, updated, store_next)
-        for g in (by_row, by_col, by_square):
-            g.sent()
-        for number, (y_, z_) in enumerate(shared):
-            share(number, y_, z_, 0, lambda copy: copy.wait_send())
         return 0
 
     lax.fori_loop(0, 2, one_step, 0)
+    square_gather(1).sent()
 
 
 def shards(pattern, matrix):
@@ -273,7 +299,7 @@
         kernel,
         name="sign_steps",
         out_shape=jax.ShapeDtypeStruct((ROWS, COLS), F32),
-        in_specs=[pl.BlockSpec(memory_space=pl.ANY), pl.BlockSpec(memory_space=pl.ANY)],
+        in_specs=[pl.BlockSpec(memory_space=pl.ANY)] * 2,
         out_specs=pl.BlockSpec(memory_space=pltpu.VMEM),
         scratch_shapes=[
             pltpu.SMEM((32, 32), jnp.int32),
@@ -284,8 +310,8 @@
             pltpu.SemaphoreType.DMA((5,)),
             pltpu.SemaphoreType.DMA((6, len(COPIES))),
             pltpu.SemaphoreType.DMA((6, len(COPIES))),
-            pltpu.SemaphoreType.DMA((2, 8, 2)),
-            pltpu.SemaphoreType.DMA((2, 8, 2)),
+            pltpu.SemaphoreType.DMA((2, 8)),
+            pltpu.SemaphoreType.DMA((2, 8)),
         ],
         compiler_params=pltpu.CompilerParams(collective_id=0, has_side_effects=True, vmem_limit_bytes=56 << 20),
         cost_estimate=pl.CostEstimate(flops=4 * 2 * 512 * 256 * 4096, bytes_accessed=1 << 20, transcendentals=0),

time: 92.1 us -> 81.8 us (0.89)
  Pallas kernels: 90 us -> 79.7 us
    pallas_call x1, Pallas kernels: 90 us -> 79.7 us  [shards(): pl.pallas_call(kernel, name='sign_steps', out_shape=jax.ShapeDtypeStruct(...]
where the time goes in v3:
time: 81.8 us; the launch traced here: 81.6 us
  Pallas kernels  79.7 us (97%)
  local copies, waits for them, and re-layouts  1.87 us (2%)
    pallas_call x1, Pallas kernels, shards(): pl.pallas_call(kernel, name='sign_steps', out_shape=jax.ShapeDtypeStruct(...  79.7 us
    unnamed x1, local copies, waits for them, and re-layouts  1.87 us

profile of v3, /device:TPU:5, one launch (start us, length us, event | category | flops | bytes accessed | tf_op | source)
XLA Modules:
  0.0 81.6 jit_solution(148127764839201969)
XLA Ops:
  0.0 79.7 %sign_steps.1 = f32[512,256]{1,0:T(8,128)} custom-call(s32[32,32]{1,0:T(8,128)} %pattern_hbm.1, bf16[512,256]{1,0:T(8,128)(2,1)} %y_hbm.1), custom_call_target="tpu_custom_call" | custom-call | flops 4294967296 | bytes 1048576 | tf_op jit(solution)/shard_map/sign_steps/pallas_call | solution.py:298
  79.7 1.9 %copy.4 = f32[512,256]{1,0:T(8,128)} copy(f32[512,256]{1,0:T(8,128)} %sign_steps.1) | data formatting | bytes 1048576

commit v4 on v3

--- a/solution.py
+++ b/solution.py
@@ -196,7 +196,7 @@
         lax.fori_loop(0, 8, at_col, 0)
 
     def product(left, right, m, places):
-        at = pl.ds(m * COLS, COLS)
+        at = pl.ds(pl.multiple_of(m * COLS, COLS), COLS)
         terms = []
         for k in places:
             for c in range(2):
@@ -209,8 +209,8 @@
         for i in range(2):
             for j in range(2):
                 keep = pattern[row * 4 + 2 * m + i, col * 2 + j].astype(F32)
-                block = value(pl.ds((2 * m + i) * BLOCK, BLOCK), i, j)
-                store(pl.ds((2 * m + i) * BLOCK, BLOCK), j, keep * block)
+                at = pl.ds(pl.multiple_of((2 * m + i) * BLOCK, BLOCK), BLOCK)
+                store(at, j, keep * value(at, i, j))
 
     def square_gather(step):
         n = 3 * step + 2
@@ -252,13 +252,17 @@
         for number, (y_, z_) in enumerate(shared):
             share(number, y_, z_, 1).wait_recv()
         scale = 1.0 / (3.0 * 4096)
-        for m in range(2):
+
+        def square_half(m, _):
             full = product(y_rows, y_cols, m, range(8))
 
             def store_square(at, j, block):
                 square[row, j, at] = block.astype(jnp.bfloat16)
 
             masked(m, lambda at, i, j: full[i * BLOCK : (i + 1) * BLOCK, j * BLOCK : (j + 1) * BLOCK] * scale, store_square)
+            return 0
+
+        lax.fori_loop(0, 2, square_half, 0)
         by_square.start(*SQUARE_OWN)
         for i in SQUARE_WAITS[:8]:
             by_square.arrived(i)
@@ -266,12 +270,27 @@
         by_col.sent()
         for number, (y_, z_) in enumerate(shared):
             share(number, y_, z_, 0).wait_send()
-        for m in range(2):
-            total[pl.ds(m * COLS, COLS)] = product(y_rows, square, m, [z_hi * 4 + k for k in range(4)])
-        for i in SQUARE_WAITS[8:]:
+
+        def near_half(m, _):
+            total[pl.ds(pl.multiple_of(m * COLS, COLS), COLS)] = product(y_rows, square, m, [z_hi * 4 + k for k in range(4)])
+            return 0
+
+        lax.fori_loop(0, 2, near_half, 0)
+        for i in SQUARE_WAITS[8:12]:
             by_square.arrived(i)
-        for m in range(2):
-            full = total[pl.ds(m * COLS, COLS)] + product(y_rows, square, m, [(1 - z_hi) * 4 + k for k in range(4)])
+
+        def side_half(m, _):
+            at = pl.ds(pl.multiple_of(m * COLS, COLS), COLS)
+            total[at] += product(y_rows, square, m, [(1 - z_hi) * 4 + ring(x + k) for k in (3, 0, 1)])
+            return 0
+
+        lax.fori_loop(0, 2, side_half, 0)
+        for i in SQUARE_WAITS[12:]:
+            by_square.arrived(i)
+
+        def far_half(m, _):
+            full = total[pl.ds(pl.multiple_of(m * COLS, COLS), COLS)]
+            full += product(y_rows, square, m, [(1 - z_hi) * 4 + ring(x + 2)])
 
             def updated(at, i, j):
                 cube = full[i * BLOCK : (i + 1) * BLOCK, j * BLOCK : (j + 1) * BLOCK]
@@ -288,6 +307,9 @@
                     out_ref[at, pl.ds(j * BLOCK, BLOCK)] = block
 
             masked(m, updated, store_next)
+            return 0
+
+        lax.fori_loop(0, 2, far_half, 0)
         return 0
 
     lax.fori_loop(0, 2, one_step, 0)
@@ -298,7 +320,7 @@
     return pl.pallas_call(
         kernel,
         name="sign_steps",
-        out_shape=jax.ShapeDtypeStruct((ROWS, COLS), F32),
+        out_shape=pltpu.VMEM((ROWS, COLS), F32),
         in_specs=[pl.BlockSpec(memory_space=pl.ANY)] * 2,
         out_specs=pl.BlockSpec(memory_space=pltpu.VMEM),
         scratch_shapes=[
@@ -313,9 +335,9 @@
             pltpu.SemaphoreType.DMA((2, 8)),
             pltpu.SemaphoreType.DMA((2, 8)),
         ],
-        compiler_params=pltpu.CompilerParams(collective_id=0, has_side_effects=True, vmem_limit_bytes=56 << 20),
+        compiler_params=pltpu.CompilerParams(collective_id=0, has_side_effects=True, vmem_limit_bytes=40 << 20),
         cost_estimate=pl.CostEstimate(flops=4 * 2 * 512 * 256 * 4096, bytes_accessed=1 << 20, transcendentals=0),
-    )(pattern, matrix)
+    )(*(pltpu.with_memory_space_constraint(a, pltpu.HBM) for a in (pattern, matrix)))
 
 
 def solution(mesh):

time: 81.8 us -> 79.4 us (0.971); the launches traced: 81.6 us -> 78.4 us
  Pallas kernels: 79.7 us -> 77.6 us
  local copies, waits for them, and re-layouts: 1.87 us -> 0.8 us
    pallas_call x1, Pallas kernels: 79.7 us -> 77.6 us  [shards(): pl.pallas_call(kernel, name='sign_steps', out_shape=pltpu.VMEM((ROWS, COL...]
    unnamed x1, local copies, waits for them, and re-layouts: 1.87 us -> 0.8 us
where the time goes in v4:
time: 79.4 us; the launch traced here: 78.4 us
  Pallas kernels  77.6 us (98%)
  local copies, waits for them, and re-layouts  0.8 us (1%)
    pallas_call x1, Pallas kernels, shards(): pl.pallas_call(kernel, name='sign_steps', out_shape=pltpu.VMEM((ROWS, COL...  77.6 us

profile of v4, /device:TPU:5, one launch (start us, length us, event | category | flops | bytes accessed | tf_op | source)
XLA Modules:
  0.0 78.4 jit_solution(9340488539208929653)
XLA Ops:
  0.0 77.6 %sign_steps.1 = f32[512,256]{1,0:T(8,128)S(1)} custom-call(s32[32,32]{1,0:T(8,128)} %pattern_hbm.1, bf16[512,256]{1,0:T(8,128)(2,1)} %y_hbm.1), custom_call_target="tpu_custom_call" | custom-call | flops 4294967296 | bytes 1048576 | tf_op jit(solution)/shard_map/sign_steps/pallas_call | solution.py:320
  77.6 0.8 %copy.4 = f32[512,256]{1,0:T(8,128)} copy(f32[512,256]{1,0:T(8,128)S(1)} %sign_steps.1) | data formatting | bytes 1048576

commit v5 on v4

--- a/solution.py
+++ b/solution.py
@@ -35,7 +35,7 @@
 AROUND = (COPIES, {0: (6,), 3: (7,), 4: (8,), 5: (11, 9, 10), 8: (12,), 11: (13,)})
 OVER = (ACROSS, {0: (6,), 3: (7,), 4: (8, 10), 5: (11, 9), 6: (12,), 7: (13,)})
 TILES = {(0, 1): (-1, 0), (2, 3): (1, 0), (4, 5): (0, 1), (6, 7): (2, 0), (8, 9): (-1, 1), (10, 11): (1, 1), (12, 13): (2, 1)}
-OWN = ("c4", "c0", "r0", "c3", "r3", "c5", "c1", "r1", "c2", "r2", "r4", "r5")
+OWN = ("c4", "r3", "c0", "r0", "c3", "c5", "c1", "r1", "c2", "r2", "r4", "r5")
 WAITS = (
     "r0", "c0", "r3", "c3", "c4", "c5", "r1", "r2", "r6", "r7", "r4", "c8", "c11", "r5",
     "r8", "r9", "r10", "r11", "r12", "r13", "c1", "c2", "c6", "c7", "c9", "c10", "c12", "c13",

time: 79.4 us -> 78.6 us (0.990)
  no operation moved by 1% of the time
where the time goes in v5:
time: 78.6 us; the launch traced here: 78.3 us
  Pallas kernels  77.5 us (99%)
  local copies, waits for them, and re-layouts  0.8 us (1%)
    pallas_call x1, Pallas kernels, shards(): pl.pallas_call(kernel, name='sign_steps', out_shape=pltpu.VMEM((ROWS, COL...  77.5 us

profile of v5, /device:TPU:5, one launch (start us, length us, event | category | flops | bytes accessed | tf_op | source)
XLA Modules:
  0.0 78.3 jit_solution(4056609754797473242)
XLA Ops:
  0.0 77.5 %sign_steps.1 = f32[512,256]{1,0:T(8,128)S(1)} custom-call(s32[32,32]{1,0:T(8,128)} %pattern_hbm.1, bf16[512,256]{1,0:T(8,128)(2,1)} %y_hbm.1), custom_call_target="tpu_custom_call" | custom-call | flops 4294967296 | bytes 1048576 | tf_op jit(solution)/shard_map/sign_steps/pallas_call | solution.py:320
  77.5 0.8 %copy.4 = f32[512,256]{1,0:T(8,128)} copy(f32[512,256]{1,0:T(8,128)S(1)} %sign_steps.1) | data formatting | bytes 1048576

commit v6 on v5

--- a/solution.py
+++ b/solution.py
@@ -84,6 +84,9 @@
         r = reach(self.cell(*owner), self.fixed)
         if self.halves is near_centre and i in SECOND:
             r = jnp.where(sender == (3 if side > 0 else 0), -1, r)
+
+        if self.halves is same_halves and 8 <= i < 12:
+            r = jnp.where(lax.rem(sender + plane, 2) == 1, -1, r)
 
         def act(width, inner):
             low, count = run(width, inner, self.core)
@@ -184,7 +187,9 @@
 
     def clear_all():
         def at_row(s, _):
-            clear((rows,), 2 * s + core, row_cell(s // 2, lax.rem(s, 2)), p, core)
+            wipe = clear((rows,), 2 * s + core, row_cell(s // 2, lax.rem(s, 2)), p, core)
+            apart = lax.rem(s // 2 + y, 2) * lax.rem(s + z_lo, 2) * lax.rem(s // 2 + z_lo, 2)
+            pl.when(apart == 1)(lambda: [wipe(j, 0, 4) for j in range(2)] and None)
             return 0
 
         def at_col(s, _):
@@ -240,6 +245,7 @@
             gathers[name[0]].start(int(name[1:]))
         pl.when(step == 0)(clear_all)
         share_start(y, z_lo)
+        pl.when(step == 1)(square_gather(0).sent)
         here = set()
         for name in WAITS:
             gathers[name[0]].arrived(int(name[1:]))
@@ -248,7 +254,6 @@
                 for parts, (offset, other) in TILES.items():
                     if int(name[1:]) in parts and here.issuperset(parts):
                         share_start(ring(y + offset), 1 - z_lo if other else z_lo)
-        pl.when(step == 1)(square_gather(0).sent)
         for number, (y_, z_) in enumerate(shared):
             share(number, y_, z_, 1).wait_recv()
         scale = 1.0 / (3.0 * 4096)

time: 78.6 us -> 78.6 us (level)
  no operation moved by 1% of the time
where the time goes in v6:
time: 78.6 us; the launch traced here: 78.2 us
  Pallas kernels  77.4 us (98%)
  local copies, waits for them, and re-layouts  0.8 us (1%)
    pallas_call x1, Pallas kernels, shards(): pl.pallas_call(kernel, name='sign_steps', out_shape=pltpu.VMEM((ROWS, COL...  77.4 us

profile of v6, /device:TPU:5, one launch (start us, length us, event | category | flops | bytes accessed | tf_op | source)
XLA Modules:
  0.0 78.2 jit_solution(17020894625016157205)
XLA Ops:
  0.0 77.4 %sign_steps.1 = f32[512,256]{1,0:T(8,128)S(1)} custom-call(s32[32,32]{1,0:T(8,128)} %pattern_hbm.1, bf16[512,256]{1,0:T(8,128)(2,1)} %y_hbm.1), custom_call_target="tpu_custom_call" | custom-call | flops 4294967296 | bytes 1048576 | tf_op jit(solution)/shard_map/sign_steps/pallas_call | solution.py:325
  77.4 0.8 %copy.4 = f32[512,256]{1,0:T(8,128)} copy(f32[512,256]{1,0:T(8,128)S(1)} %sign_steps.1) | data formatting | bytes 1048576
